TPU v7x, 32 devices: a whole 2x2x4 slice. The times are simulated.
32 devices in a mesh: clip: 16 (over z, y, core), row: 2 (over x).
Axes of the slice: x: 2, y: 2, z: 4, core: 2. Of those that a mesh axis runs over, the one named last changes fastest.
Arguments:
- video: bfloat16 [64, 16, 320, 128], P('clip', 'row'), may hold values from -6 to 6
- spatial_one: bfloat16 [3, 3, 320, 320], replicated, may hold values from -0.109375 to 0.109375
- spatial_two: bfloat16 [3, 3, 320, 320], replicated, may hold values from -0.109375 to 0.109375
- temporal_mix: bfloat16 [3, 320, 320], replicated, may hold values from -0.1875 to 0.1875
- bias_one: float32 [320], replicated, may hold values from -3 to 3
- bias_two: float32 [320], replicated, may hold values from -3 to 3
- bias_three: float32 [320], replicated, may hold values from -3 to 3
Outputs:
- block_out: bfloat16 [64, 16, 320, 128], P('clip', 'row')
All inputs are finite; a program needn't handle non-finite values.
Results may differ from a plain program's by a relative error of at most 0.011.
Values may be sent and summed in bfloat16 or wider, within the bound.
A program may use at most 128 MiB of HBM per device.

v0:
```python
import jax
import jax.numpy as jnp
from jax import lax
from jax.sharding import PartitionSpec as P


def padded(x, sides, width):
    for axis, dim in sides:
        size, length = (lax.axis_size(axis), x.shape[dim])
        up = [(i, (i + 1) % size) for i in range(size - 1)]
        down = [(j, i) for i, j in up]
        last = lax.slice_in_dim(x, length - width, length, axis=dim)
        first = lax.slice_in_dim(x, 0, width, axis=dim)
        before = lax.ppermute(last, axis, up)
        after = lax.ppermute(first, axis, down)
        x = jnp.concatenate([before, x, after], axis=dim)
    return x


def silu_round(values):
    return jax.nn.silu(values.astype(jnp.float32)).astype(jnp.bfloat16)


def conv_rows(activated, kernel):
    row_count = activated.shape[1] - 2
    partials = []
    for column_tap in range(3):
        partial_value = None
        for row_tap in range(3):
            product = jnp.einsum(
                "oc,frcw->frow",
                kernel[row_tap, column_tap],
                activated[:, row_tap : row_tap + row_count],
                preferred_element_type=jnp.float32,
            )
            partial_value = product if partial_value is None else partial_value + product
        partials.append(partial_value)
    zero_col = jnp.zeros(partials[0].shape[:-1] + (1,), jnp.float32)
    shifted_in = jnp.concatenate([zero_col, partials[0][..., :-1]], axis=3)
    shifted_out = jnp.concatenate([partials[2][..., 1:], zero_col], axis=3)
    return shifted_in + partials[1] + shifted_out


def residual_add(residual_in, bias_vec, convolved):
    return (residual_in.astype(jnp.float32) + bias_vec[:, None] + convolved).astype(jnp.bfloat16)


def spatial_chain(frames, spatial_one, spatial_two, bias_one, bias_two):

    def rimmed(activated):
        return padded(activated, (("row", 1),), 1)

    first_out = residual_add(frames, bias_one, conv_rows(rimmed(silu_round(frames)), spatial_one))
    second = residual_add(
        first_out, bias_two, conv_rows(rimmed(silu_round(first_out)), spatial_two)
    )
    return second


def body(video, spatial_one, spatial_two, temporal_mix, bias_one, bias_two, bias_three):
    frame_count = video.shape[0]
    centre = spatial_chain(video, spatial_one, spatial_two, bias_one, bias_two)
    activated = padded(silu_round(centre), (("clip", 0),), 1)
    mixed_out = centre.astype(jnp.float32) + bias_three[:, None]
    for frame_tap in range(3):
        mixed_out = mixed_out + jnp.einsum(
            "oc,frcw->frow",
            temporal_mix[frame_tap],
            activated[frame_tap : frame_tap + frame_count],
            preferred_element_type=jnp.float32,
        )
    return mixed_out.astype(jnp.bfloat16)


def solution(mesh):
    placed = (P("clip", "row", None, None), P(), P(), P(), P(), P(), P())
    return jax.shard_map(
        body, mesh=mesh, in_specs=placed, out_specs=P("clip", "row", None, None), check_vma=False
    )
```

profile of v0, /device:TPU:14, one launch (start us, length us, event | category | flops | bytes accessed | tf_op | source)
XLA Modules:
  0.0 97.1 jit_solution(12981858234257832171)
XLA Ops:
  0.0 3.2 %fusion.5 = bf16[4,8,320,128]{3,2,1,0:T(8,128)(2,1)S(1)} fusion(bf16[4,8,320,128]{3,2,1,0:T(8,128)(2,1)} %param.7), kind=kLoop, calls=%fused_computation.14 | loop fusion | flops 7864320 | bytes 5242880 | tf_op jit(solution)/shard_map/convert_element_type | solution.py:21
  3.3 2.5 %collective-permute-start.1 = (bf16[4,1,320,128]{3,2,1,0:T(8,128)(2,1)S(1)}, bf16[4,1,320,128]{3,2,1,0:T(8,128)(2,1)S(1)}, u32[]{:S(2)}, u32[]{:S(2)}) collective-permute-start(bf16[4,1,320,128]{3,2,1,0:T(8,128)(2,1)S(1)} %get-tuple-element.9), channel_id=1, source_target_pairs={{1,0},{3,2},{5,4},{7,6},{9,8},{11,10},{13,12},{15,14},{17,16},{19,... | collective-permute-start | bytes 983048 | tf_op jit(solution)/shard_map/ppermute | solution.py:15
  5.8 1.3 %collective-permute-start = (bf16[4,1,320,128]{3,2,1,0:T(8,128)(2,1)S(1)}, bf16[4,1,320,128]{3,2,1,0:T(8,128)(2,1)S(1)}, u32[]{:S(2)}, u32[]{:S(2)}) collective-permute-start(bf16[4,1,320,128]{3,2,1,0:T(8,128)(2,1)S(1)} %get-tuple-element.10), channel_id=1, source_target_pairs={{0,1},{2,3},{4,5},{6,7},{8,9},{10,11},{12,13},{14,15},{16,17},{18,... | collective-permute-start | bytes 983048 | tf_op jit(solution)/shard_map/ppermute | solution.py:14
  7.1 0.0 copy-done.1
  7.1 1.5 %fusion.63 = f32[4,8,128,320]{2,3,1,0:T(8,128)S(1)} fusion(bf16[4,8,320,128]{3,2,1,0:T(8,128)(2,1)S(1)} %fusion.5, bf16[3,3,320,320]{3,2,1,0:T(8,128)(2,1)S(1)} %copy-done.1), kind=kOutput, calls=%fused_computation.84 | convolution fusion | flops 838860800 | bytes 8110080 | tf_op jit(solution)/shard_map/oc,frcw->frow/dot_general | solution.py:30
  8.6 1.5 %fusion.59 = f32[4,8,128,320]{2,3,1,0:T(8,128)S(1)} fusion(bf16[4,8,320,128]{3,2,1,0:T(8,128)(2,1)S(1)} %fusion.5, bf16[3,3,320,320]{3,2,1,0:T(8,128)(2,1)S(1)} %copy-done.1), kind=kOutput, calls=%fused_computation.80 | convolution fusion | flops 838860800 | bytes 8110080 | tf_op jit(solution)/shard_map/oc,frcw->frow/dot_general | solution.py:30
  10.1 1.5 %fusion.55 = f32[4,8,128,320]{2,3,1,0:T(8,128)S(1)} fusion(bf16[4,8,320,128]{3,2,1,0:T(8,128)(2,1)S(1)} %fusion.5, bf16[3,3,320,320]{3,2,1,0:T(8,128)(2,1)S(1)} %copy-done.1), kind=kOutput, calls=%fused_computation.76 | convolution fusion | flops 838860800 | bytes 8110080 | tf_op jit(solution)/shard_map/oc,frcw->frow/dot_general | solution.py:30
  11.7 5.2 %collective-permute-done = bf16[4,1,320,128]{3,2,1,0:T(8,128)(2,1)S(1)} collective-permute-done((bf16[4,1,320,128]{3,2,1,0:T(8,128)(2,1)S(1)}, bf16[4,1,320,128]{3,2,1,0:T(8,128)(2,1)S(1)}, u32[]{:S(2)}, u32[]{:S(2)}) %collective-permute-start) | collective-permute-done | bytes 327712 | tf_op jit(solution)/shard_map/ppermute | solution.py:14
  16.8 1.5 %fusion.27 = f32[4,8,128,320]{2,3,1,0:T(8,128)S(1)} fusion(bf16[4,8,320,128]{3,2,1,0:T(8,128)(2,1)S(1)} %fusion.5, bf16[4,1,320,128]{3,2,1,0:T(8,128)(2,1)S(1)} %collective-permute-done, bf16[3,3,320,320]{3,2,1,0:T(8,128)(2,1)S(1)} %copy-done.1), kind=kOutput, calls=%fused_computation.48 | convolution fusion | flops 844103680 | bytes 8437760 | tf_op jit(solution)/shard_map/oc,frcw->frow/dot_general | solution.py:30
  18.4 0.0 collective-permute-done.1
  18.4 0.0 copy-start.4
  18.4 1.6 %add_bitcast_fusion.2 = f32[4,8,320,128]{3,2,1,0:T(8,128)S(1)} fusion(f32[4,8,128,320]{2,3,1,0:T(8,128)S(1)} %fusion.27, f32[4,8,128,320]{2,3,1,0:T(8,128)S(1)} %fusion.55, bf16[4,1,320,128]{3,2,1,0:T(8,128)(2,1)S(1)} %collective-permute-done.1, bf16[4,8,320,128]{3,2,1,0:T(8,128)(2,1)S(1)} %fusion.5, bf16[3,3,320,320]{3,2,1,0:T(8,128)(2,1)S(1)} %copy-done.1), kind=kOutput, calls=%fused_computation.35 | convolution fusion | flops 846725120 | bytes 18923520 | tf_op jit(solution)/shard_map/oc,frcw->frow/dot_general | solution.py:30
  20.0 1.4 %slice.165 = f32[4,8,320,127]{3,2,1,0:T(8,128)S(1)} slice(f32[4,8,320,128]{3,2,1,0:T(8,128)S(1)} %add_bitcast_fusion.2), slice={[0:4], [0:8], [0:320], [1:128]} | slice | bytes 10403840 | tf_op jit(solution)/shard_map/slice | solution.py:40
  21.4 2.5 %fusion.26 = f32[4,8,128,320]{2,3,1,0:T(8,128)S(1)} fusion(bf16[4,8,320,128]{3,2,1,0:T(8,128)(2,1)S(1)} %fusion.5, bf16[4,1,320,128]{3,2,1,0:T(8,128)(2,1)S(1)} %collective-permute-done, bf16[3,3,320,320]{3,2,1,0:T(8,128)(2,1)} %param.8), kind=kOutput, calls=%fused_computation.47 | convolution fusion | flops 844103680 | bytes 8437760 | tf_op jit(solution)/shard_map/oc,frcw->frow/dot_general | solution.py:30
  23.9 2.5 %fusion.28 = f32[4,8,128,320]{2,3,1,0:T(8,128)S(1)} fusion(bf16[4,8,320,128]{3,2,1,0:T(8,128)(2,1)S(1)} %fusion.5, bf16[4,1,320,128]{3,2,1,0:T(8,128)(2,1)S(1)} %collective-permute-done, bf16[3,3,320,320]{3,2,1,0:T(8,128)(2,1)} %param.8), kind=kOutput, calls=%fused_computation.49 | convolution fusion | flops 844103680 | bytes 8437760 | tf_op jit(solution)/shard_map/oc,frcw->frow/dot_general | solution.py:30
  26.4 0.0 copy-done.4
  26.4 0.0 copy-start.7
  26.4 4.9 %add_bitcast_fusion.3 = f32[4,8,320,128]{3,2,1,0:T(8,128)} fusion(f32[4,8,128,320]{2,3,1,0:T(8,128)S(1)} %fusion.28, f32[4,8,128,320]{2,3,1,0:T(8,128)S(1)} %fusion.63, bf16[4,1,320,128]{3,2,1,0:T(8,128)(2,1)S(1)} %collective-permute-done.1, bf16[4,8,320,128]{3,2,1,0:T(8,128)(2,1)S(1)} %fusion.5, bf16[3,3,320,320]{3,2,1,0:T(8,128)(2,1)} %param.8), kind=kOutput, calls=%fused_computation.36 | convolution fusion | flops 846725120 | bytes 18923520 | tf_op jit(solution)/shard_map/oc,frcw->frow/dot_general | solution.py:30
  31.3 7.3 %fusion.11 = (bf16[4,8,320,128]{3,2,1,0:T(8,128)(2,1)S(1)}, bf16[4,8,320,128]{3,2,1,0:T(8,128)(2,1)}) fusion(f32[4,8,320,127]{3,2,1,0:T(8,128)S(1)} %slice.165, bf16[4,1,320,128]{3,2,1,0:T(8,128)(2,1)} %copy-done.4, bf16[4,8,320,128]{3,2,1,0:T(8,128)(2,1)S(1)} %fusion.5, bf16[3,3,320,320]{3,2,1,0:T(8,128)(2,1)} %param.8, ...), kind=kOutput, calls=%fused_computation.20 | convolution fusion | flops 862453760 | bytes 31991040 | tf_op jit(solution)/shard_map/oc,frcw->frow/dot_general | solution.py:30
  38.6 0.0 copy-start.2
  38.7 2.6 %fusion.51 = f32[4,8,128,320]{2,3,1,0:T(8,128)S(1)} fusion(bf16[4,8,320,128]{3,2,1,0:T(8,128)(2,1)S(1)} %get-tuple-element.11, bf16[3,3,320,320]{3,2,1,0:T(8,128)(2,1)} %param.9), kind=kOutput, calls=%fused_computation.72 | convolution fusion | flops 838860800 | bytes 8110080 | tf_op jit(solution)/shard_map/oc,frcw->frow/dot_general | solution.py:30
  41.3 0.0 copy-done.2
  41.3 1.5 %fusion.47 = f32[4,8,128,320]{2,3,1,0:T(8,128)S(1)} fusion(bf16[4,8,320,128]{3,2,1,0:T(8,128)(2,1)S(1)} %get-tuple-element.11, bf16[3,3,320,320]{3,2,1,0:T(8,128)(2,1)S(1)} %copy-done.2), kind=kOutput, calls=%fused_computation.68 | convolution fusion | flops 838860800 | bytes 8110080 | tf_op jit(solution)/shard_map/oc,frcw->frow/dot_general | solution.py:30
  42.9 1.5 %collective-permute-start.3 = (bf16[4,1,320,128]{3,2,1,0:T(8,128)(2,1)S(1)}, bf16[4,1,320,128]{3,2,1,0:T(8,128)(2,1)S(1)}, u32[]{:S(2)}, u32[]{:S(2)}) collective-permute-start(bf16[4,1,320,128]{3,2,1,0:T(8,128)(2,1)S(1)} %get-tuple-element.7), channel_id=1, source_target_pairs={{1,0},{3,2},{5,4},{7,6},{9,8},{11,10},{13,12},{15,14},{17,16},{19,... | collective-permute-start | bytes 983048 | tf_op jit(solution)/shard_map/ppermute | solution.py:15
  44.3 1.3 %collective-permute-start.2 = (bf16[4,1,320,128]{3,2,1,0:T(8,128)(2,1)S(1)}, bf16[4,1,320,128]{3,2,1,0:T(8,128)(2,1)S(1)}, u32[]{:S(2)}, u32[]{:S(2)}) collective-permute-start(bf16[4,1,320,128]{3,2,1,0:T(8,128)(2,1)S(1)} %get-tuple-element.8), channel_id=1, source_target_pairs={{0,1},{2,3},{4,5},{6,7},{8,9},{10,11},{12,13},{14,15},{16,17},{18,... | collective-permute-start | bytes 983048 | tf_op jit(solution)/shard_map/ppermute | solution.py:14
  45.6 1.5 %fusion.43 = f32[4,8,128,320]{2,3,1,0:T(8,128)S(1)} fusion(bf16[4,8,320,128]{3,2,1,0:T(8,128)(2,1)S(1)} %get-tuple-element.11, bf16[3,3,320,320]{3,2,1,0:T(8,128)(2,1)S(1)} %copy-done.2), kind=kOutput, calls=%fused_computation.64 | convolution fusion | flops 838860800 | bytes 8110080 | tf_op jit(solution)/shard_map/oc,frcw->frow/dot_general | solution.py:30
  47.2 7.1 %collective-permute-done.2 = bf16[4,1,320,128]{3,2,1,0:T(8,128)(2,1)S(1)} collective-permute-done((bf16[4,1,320,128]{3,2,1,0:T(8,128)(2,1)S(1)}, bf16[4,1,320,128]{3,2,1,0:T(8,128)(2,1)S(1)}, u32[]{:S(2)}, u32[]{:S(2)}) %collective-permute-start.2) | collective-permute-done | bytes 327712 | tf_op jit(solution)/shard_map/ppermute | solution.py:14
  54.3 1.5 %fusion.33 = f32[4,8,128,320]{2,3,1,0:T(8,128)S(1)} fusion(bf16[4,8,320,128]{3,2,1,0:T(8,128)(2,1)S(1)} %get-tuple-element.11, bf16[4,1,320,128]{3,2,1,0:T(8,128)(2,1)S(1)} %collective-permute-done.2, bf16[3,3,320,320]{3,2,1,0:T(8,128)(2,1)S(1)} %copy-done.2), kind=kOutput, calls=%fused_computation.54 | convolution fusion | flops 844103680 | bytes 8437760 | tf_op jit(solution)/shard_map/oc,frcw->frow/dot_general | solution.py:30
  55.9 0.0 collective-permute-done.3
  55.9 0.0 copy-start.3
  55.9 1.8 %add_bitcast_fusion = f32[4,8,320,128]{3,2,1,0:T(8,128)S(1)} fusion(f32[4,8,128,320]{2,3,1,0:T(8,128)S(1)} %fusion.33, f32[4,8,128,320]{2,3,1,0:T(8,128)S(1)} %fusion.43, bf16[4,1,320,128]{3,2,1,0:T(8,128)(2,1)S(1)} %collective-permute-done.3, bf16[4,8,320,128]{3,2,1,0:T(8,128)(2,1)S(1)} %get-tuple-element.11, bf16[3,3,320,320]{3,2,1,0:T(8,128)(2,1)S(1)} %copy-done.2), kind=kOutput, calls=%fused_computation.33 | convolution fusion | flops 846725120 | bytes 18923520 | tf_op jit(solution)/shard_map/oc,frcw->frow/dot_general | solution.py:30
  57.7 1.4 %slice.169 = f32[4,8,320,127]{3,2,1,0:T(8,128)S(1)} slice(f32[4,8,320,128]{3,2,1,0:T(8,128)S(1)} %add_bitcast_fusion), slice={[0:4], [0:8], [0:320], [1:128]} | slice | bytes 10403840 | tf_op jit(solution)/shard_map/slice | solution.py:40
  59.1 1.5 %fusion.32 = f32[4,8,128,320]{2,3,1,0:T(8,128)S(1)} fusion(bf16[4,8,320,128]{3,2,1,0:T(8,128)(2,1)S(1)} %get-tuple-element.11, bf16[4,1,320,128]{3,2,1,0:T(8,128)(2,1)S(1)} %collective-permute-done.2, bf16[3,3,320,320]{3,2,1,0:T(8,128)(2,1)S(1)} %copy-done.2), kind=kOutput, calls=%fused_computation.53 | convolution fusion | flops 844103680 | bytes 8437760 | tf_op jit(solution)/shard_map/oc,frcw->frow/dot_general | solution.py:30
  60.6 1.5 %fusion.34 = f32[4,8,128,320]{2,3,1,0:T(8,128)S(1)} fusion(bf16[4,8,320,128]{3,2,1,0:T(8,128)(2,1)S(1)} %get-tuple-element.11, bf16[4,1,320,128]{3,2,1,0:T(8,128)(2,1)S(1)} %collective-permute-done.2, bf16[3,3,320,320]{3,2,1,0:T(8,128)(2,1)S(1)} %copy-done.2), kind=kOutput, calls=%fused_computation.55 | convolution fusion | flops 844103680 | bytes 8437760 | tf_op jit(solution)/shard_map/oc,frcw->frow/dot_general | solution.py:30
  62.2 0.0 copy-start.8
  62.2 3.9 %add_bitcast_fusion.1 = f32[4,8,320,128]{3,2,1,0:T(8,128)} fusion(f32[4,8,128,320]{2,3,1,0:T(8,128)S(1)} %fusion.34, f32[4,8,128,320]{2,3,1,0:T(8,128)S(1)} %fusion.51, bf16[4,1,320,128]{3,2,1,0:T(8,128)(2,1)S(1)} %collective-permute-done.3, bf16[4,8,320,128]{3,2,1,0:T(8,128)(2,1)S(1)} %get-tuple-element.11, bf16[3,3,320,320]{3,2,1,0:T(8,128)(2,1)S(1)} %copy-done.2), kind=kOutput, calls=%fused_computation.34 | convolution fusion | flops 846725120 | bytes 18923520 | tf_op jit(solution)/shard_map/oc,frcw->frow/dot_general | solution.py:30
  66.1 0.0 copy-done.8
  66.1 7.3 %fusion.19 = (bf16[4,8,320,128]{3,2,1,0:T(8,128)(2,1)S(1)}, bf16[4,8,320,128]{3,2,1,0:T(8,128)(2,1)}) fusion(f32[4,8,320,127]{3,2,1,0:T(8,128)S(1)} %slice.169, bf16[4,1,320,128]{3,2,1,0:T(8,128)(2,1)} %copy-done.3, bf16[4,8,320,128]{3,2,1,0:T(8,128)(2,1)S(1)} %get-tuple-element.11, bf16[3,3,320,320]{3,2,1,0:T(8,128)(2,1)} %param.9, ...), kind=kOutput, calls=%fused_computation.28 | convolution fusion | flops 862453760 | bytes 31991040 | tf_op jit(solution)/shard_map/oc,frcw->frow/dot_general | solution.py:30
  73.4 0.1 fusion.101
  73.5 2.1 %collective-permute-start.4 = (bf16[1,8,320,128]{3,2,1,0:T(8,128)(2,1)S(1)}, bf16[1,8,320,128]{3,2,1,0:T(8,128)(2,1)S(1)}, u32[]{:S(2)}, u32[]{:S(2)}) collective-permute-start(bf16[1,8,320,128]{3,2,1,0:T(8,128)(2,1)S(1)} %get-tuple-element.6), channel_id=1, source_target_pairs={{0,2},{2,4},{4,6},{6,8},{8,10},{10,12},{12,14},{14,16},{16,18},{18... | collective-permute-start | bytes 1966088 | tf_op jit(solution)/shard_map/ppermute | solution.py:14
  75.5 3.9 %collective-permute-start.5 = (bf16[1,8,320,128]{3,2,1,0:T(8,128)(2,1)S(1)}, bf16[1,8,320,128]{3,2,1,0:T(8,128)(2,1)S(1)}, u32[]{:S(2)}, u32[]{:S(2)}) collective-permute-start(bf16[1,8,320,128]{3,2,1,0:T(8,128)(2,1)S(1)} %get-tuple-element.5), channel_id=1, source_target_pairs={{2,0},{4,2},{6,4},{8,6},{10,8},{12,10},{14,12},{16,14},{18,16},{20... | collective-permute-start | bytes 1966088 | tf_op jit(solution)/shard_map/ppermute | solution.py:15
  79.4 1.5 %fusion.39 = f32[4,8,128,320]{2,3,1,0:T(8,128)S(1)} fusion(bf16[4,8,320,128]{3,2,1,0:T(8,128)(2,1)S(1)} %get-tuple-element.13, bf16[3,320,320]{2,1,0:T(8,128)(2,1)S(1)} %copy-done.5), kind=kOutput, calls=%fused_computation.60 | convolution fusion | flops 838860800 | bytes 8110080 | tf_op jit(solution)/shard_map/oc,frcw->frow/dot_general | solution.py:66
  80.9 0.0 copy-start
  81.0 0.0 copy-start.6
  81.0 11.5 %collective-permute-done.4 = bf16[1,8,320,128]{3,2,1,0:T(8,128)(2,1)S(1)} collective-permute-done((bf16[1,8,320,128]{3,2,1,0:T(8,128)(2,1)S(1)}, bf16[1,8,320,128]{3,2,1,0:T(8,128)(2,1)S(1)}, u32[]{:S(2)}, u32[]{:S(2)}) %collective-permute-start.4) | collective-permute-done | bytes 655392 | tf_op jit(solution)/shard_map/ppermute | solution.py:14
  92.5 1.5 %fusion.24 = f32[4,8,128,320]{2,3,1,0:T(8,128)S(1)} fusion(bf16[4,8,320,128]{3,2,1,0:T(8,128)(2,1)S(1)} %get-tuple-element.13, bf16[1,8,320,128]{3,2,1,0:T(8,128)(2,1)S(1)} %collective-permute-done.4, bf16[3,320,320]{2,1,0:T(8,128)(2,1)S(1)} %copy-done.5), kind=kOutput, calls=%fused_computation.41 | convolution fusion | flops 844103680 | bytes 8765440 | tf_op jit(solution)/shard_map/oc,frcw->frow/dot_general | solution.py:66
  94.1 0.0 collective-permute-done.5
  94.1 3.0 %fusion.15 = bf16[4,8,320,128]{3,2,1,0:T(8,128)(2,1)} fusion(bf16[4,8,320,128]{3,2,1,0:T(8,128)(2,1)S(1)} %copy-done, f32[4,8,128,320]{2,3,1,0:T(8,128)S(1)} %fusion.39, f32[4,8,128,320]{2,3,1,0:T(8,128)S(1)} %fusion.24, f32[320]{0:T(512)S(1)} %copy-done.6, bf16[1,8,320,128]{3,2,1,0:T(8,128)(2,1)S(1)} %collective-permute-done.5, ...), kind=kOutput, calls=%fused_computation.24 | convolution fusion | flops 851968000 | bytes 19253248 | tf_op jit(solution)/shard_map/oc,frcw->frow/dot_general | solution.py:66
  (9 shorter events, 0.1 us)
Async XLA Ops:
  0.0 7.1 %copy-start.1 = (bf16[3,3,320,320]{3,2,1,0:T(8,128)(2,1)S(1)}, bf16[3,3,320,320]{3,2,1,0:T(8,128)(2,1)}, u32[]{:S(2)}) copy-start(bf16[3,3,320,320]{3,2,1,0:T(8,128)(2,1)} %param.8) | copy-start | bytes 5529604
  3.3 15.1 %collective-permute-start.1 = (bf16[4,1,320,128]{3,2,1,0:T(8,128)(2,1)S(1)}, bf16[4,1,320,128]{3,2,1,0:T(8,128)(2,1)S(1)}, u32[]{:S(2)}, u32[]{:S(2)}) collective-permute-start(bf16[4,1,320,128]{3,2,1,0:T(8,128)(2,1)S(1)} %get-tuple-element.9), channel_id=1, source_target_pairs={{1,0},{3,2},{5,4},{7,6},{9,8},{11,10},{13,12},{15,14},{17,16},{19,... | collective-permute-start | bytes 983048 | tf_op jit(solution)/shard_map/ppermute | solution.py:15
  5.8 11.1 %collective-permute-start = (bf16[4,1,320,128]{3,2,1,0:T(8,128)(2,1)S(1)}, bf16[4,1,320,128]{3,2,1,0:T(8,128)(2,1)S(1)}, u32[]{:S(2)}, u32[]{:S(2)}) collective-permute-start(bf16[4,1,320,128]{3,2,1,0:T(8,128)(2,1)S(1)} %get-tuple-element.10), channel_id=1, source_target_pairs={{0,1},{2,3},{4,5},{6,7},{8,9},{10,11},{12,13},{14,15},{16,17},{18,... | collective-permute-start | bytes 983048 | tf_op jit(solution)/shard_map/ppermute | solution.py:14
  18.4 8.0 %copy-start.4 = (bf16[4,1,320,128]{3,2,1,0:T(8,128)(2,1)}, bf16[4,1,320,128]{3,2,1,0:T(8,128)(2,1)S(1)}, u32[]{:S(2)}) copy-start(bf16[4,1,320,128]{3,2,1,0:T(8,128)(2,1)S(1)} %collective-permute-done.1) | copy-start | bytes 983044
  26.4 4.9 %copy-start.7 = (f32[320]{0:T(512)S(1)}, f32[320]{0:T(512)}, u32[]{:S(2)}) copy-start(f32[320]{0:T(512)} %param.11) | copy-start | bytes 3844
  38.6 2.7 %copy-start.2 = (bf16[3,3,320,320]{3,2,1,0:T(8,128)(2,1)S(1)}, bf16[3,3,320,320]{3,2,1,0:T(8,128)(2,1)}, u32[]{:S(2)}) copy-start(bf16[3,3,320,320]{3,2,1,0:T(8,128)(2,1)} %param.9) | copy-start | bytes 5529604
  42.9 13.0 %collective-permute-start.3 = (bf16[4,1,320,128]{3,2,1,0:T(8,128)(2,1)S(1)}, bf16[4,1,320,128]{3,2,1,0:T(8,128)(2,1)S(1)}, u32[]{:S(2)}, u32[]{:S(2)}) collective-permute-start(bf16[4,1,320,128]{3,2,1,0:T(8,128)(2,1)S(1)} %get-tuple-element.7), channel_id=1, source_target_pairs={{1,0},{3,2},{5,4},{7,6},{9,8},{11,10},{13,12},{15,14},{17,16},{19,... | collective-permute-start | bytes 983048 | tf_op jit(solution)/shard_map/ppermute | solution.py:15
  44.3 10.0 %collective-permute-start.2 = (bf16[4,1,320,128]{3,2,1,0:T(8,128)(2,1)S(1)}, bf16[4,1,320,128]{3,2,1,0:T(8,128)(2,1)S(1)}, u32[]{:S(2)}, u32[]{:S(2)}) collective-permute-start(bf16[4,1,320,128]{3,2,1,0:T(8,128)(2,1)S(1)} %get-tuple-element.8), channel_id=1, source_target_pairs={{0,1},{2,3},{4,5},{6,7},{8,9},{10,11},{12,13},{14,15},{16,17},{18,... | collective-permute-start | bytes 983048 | tf_op jit(solution)/shard_map/ppermute | solution.py:14
  55.9 6.3 %copy-start.3 = (bf16[4,1,320,128]{3,2,1,0:T(8,128)(2,1)}, bf16[4,1,320,128]{3,2,1,0:T(8,128)(2,1)S(1)}, u32[]{:S(2)}) copy-start(bf16[4,1,320,128]{3,2,1,0:T(8,128)(2,1)S(1)} %collective-permute-done.3) | copy-start | bytes 983044
  62.2 3.9 %copy-start.8 = (f32[320]{0:T(512)S(1)}, f32[320]{0:T(512)}, u32[]{:S(2)}) copy-start(f32[320]{0:T(512)} %param.12) | copy-start | bytes 3844
  73.4 6.0 %copy-start.5 = (bf16[3,320,320]{2,1,0:T(8,128)(2,1)S(1)}, bf16[3,320,320]{2,1,0:T(8,128)(2,1)}, u32[]{:S(2)}) copy-start(bf16[3,320,320]{2,1,0:T(8,128)(2,1)} %param.10) | copy-start | bytes 1843204
  73.5 19.1 %collective-permute-start.4 = (bf16[1,8,320,128]{3,2,1,0:T(8,128)(2,1)S(1)}, bf16[1,8,320,128]{3,2,1,0:T(8,128)(2,1)S(1)}, u32[]{:S(2)}, u32[]{:S(2)}) collective-permute-start(bf16[1,8,320,128]{3,2,1,0:T(8,128)(2,1)S(1)} %get-tuple-element.6), channel_id=1, source_target_pairs={{0,2},{2,4},{4,6},{6,8},{8,10},{10,12},{12,14},{14,16},{16,18},{18... | collective-permute-start | bytes 1966088 | tf_op jit(solution)/shard_map/ppermute | solution.py:14
  75.5 18.5 %collective-permute-start.5 = (bf16[1,8,320,128]{3,2,1,0:T(8,128)(2,1)S(1)}, bf16[1,8,320,128]{3,2,1,0:T(8,128)(2,1)S(1)}, u32[]{:S(2)}, u32[]{:S(2)}) collective-permute-start(bf16[1,8,320,128]{3,2,1,0:T(8,128)(2,1)S(1)} %get-tuple-element.5), channel_id=1, source_target_pairs={{2,0},{4,2},{6,4},{8,6},{10,8},{12,10},{14,12},{16,14},{18,16},{20... | collective-permute-start | bytes 1966088 | tf_op jit(solution)/shard_map/ppermute | solution.py:15
  80.9 13.1 %copy-start = (bf16[4,8,320,128]{3,2,1,0:T(8,128)(2,1)S(1)}, bf16[4,8,320,128]{3,2,1,0:T(8,128)(2,1)}, u32[]{:S(2)}) copy-start(bf16[4,8,320,128]{3,2,1,0:T(8,128)(2,1)} %get-tuple-element.14) | copy-start | bytes 7864324
  81.0 13.1 %copy-start.6 = (f32[320]{0:T(512)S(1)}, f32[320]{0:T(512)}, u32[]{:S(2)}) copy-start(f32[320]{0:T(512)} %param.13) | copy-start | bytes 3844
where the time goes:
time: 97.4 us; the launch traced here: 97.1 us
  matrix products  54.2 us (56%)
  waiting for transfers between devices  23.9 us (25%)
  starting transfers between devices  12.4 us (13%)
  other arithmetic  3.25 us (3%)
  local copies, waits for them, and re-layouts  3.05 us (3%)
    dot_general x18, matrix products, conv_rows(): jnp.einsum('oc,frcw->frow', kernel[row_tap, column_tap], activated[:, row...  48.1 us
    ppermute x3, waiting for transfers between devices, padded(): before = lax.ppermute(last, axis, up)  23.9 us
    ppermute x3, starting transfers between devices, padded(): after = lax.ppermute(first, axis, down)  7.79 us
    dot_general x3, matrix products, body(): jnp.einsum('oc,frcw->frow', temporal_mix[frame_tap], activated[frame_tap:...  6.08 us
    ppermute x3, starting transfers between devices, padded(): before = lax.ppermute(last, axis, up)  4.64 us
    convert_element_type x1, other arithmetic, silu_round(): return jax.nn.silu(values.astype(jnp.float32)).astype(jnp.bfloat16)  3.25 us
    slice x2, local copies, waits for them, and re-layouts, conv_rows(): shifted_out = jnp.concatenate([partials[2][..., 1:], zero_col], axis=3)  2.83 us
  transfers between devices with their start and end apart: 6, of which 3 were waited for; matrix products, arithmetic and copies ran while one was open for 13% of the time, Pallas kernels for 0%

commit v1 on v0

v1 whole, which is shorter than its diff:
```python
import functools

import jax
import jax.numpy as jnp
from jax import lax
from jax.experimental import pallas as pl
from jax.experimental.pallas import tpu as pltpu
from jax.sharding import PartitionSpec as P

BF16, F32 = jnp.bfloat16, jnp.float32
MESH = pl.DeviceIdType.MESH
PARTS = 2


def silu(v):
    half = 0.5 * v
    return half + half * jnp.tanh(half)


def kernel(
    clips, bands, video, w_one, w_two, w_mix, b_one, b_two, b_three, out,
    raw_one, raw_two, raw_mix, mat_one, mat_two, mat_mix, cols, x, act_one, act_two, act_three,
    w_sem, x_sem, o_sem, row_send, row_recv, clip_send, clip_recv,
):
    frames, half, c, wide = x.shape
    w = wide // 2
    n = c // PARTS
    clip, band = lax.axis_index("clip"), lax.axis_index("row")
    has_up, has_down = band > 0, band < bands - 1
    has_prev, has_next = clip > 0, clip < clips - 1
    first = jnp.where(lax.rem(clip, 2) == 0, 0, frames - 1)
    order = [first, frames - 1 - first] + list(range(1, frames - 1))

    loads_one = [pltpu.make_async_copy(w_one.at[:, j], raw_one.at[:, j], w_sem.at[j]) for j in range(3)]
    load_two = pltpu.make_async_copy(w_two, raw_two, w_sem.at[3])
    load_mix = pltpu.make_async_copy(w_mix, raw_mix, w_sem.at[4])

    def load_x(f):
        return [
            pltpu.make_async_copy(
                video.at[f, pl.ds(k * half, half)], x.at[f, :, :, pl.ds(k * w, w)], x_sem.at[f, k])
            for k in range(2)
        ]

    def start_all(copies):
        for copy in copies:
            copy.start()

    start_all(load_x(order[0]))
    start_all(loads_one)
    for f in order[1:]:
        start_all(load_x(f))
    load_two.start()
    load_mix.start()

    barrier = pltpu.get_barrier_semaphore()
    neighbours = (
        (has_up, {"row": band - 1}), (has_down, {"row": band + 1}),
        (has_prev, {"clip": clip - 1}), (has_next, {"clip": clip + 1}),
    )

    def where_to(place):
        return (place.get("clip", clip), place.get("row", band))

    for there, place in neighbours:
        @pl.when(there)
        def _():
            pl.semaphore_signal(barrier, inc=1, device_id=where_to(place), device_id_type=MESH)
    pl.semaphore_wait(barrier, sum(there.astype(jnp.int32) for there, _place in neighbours))

    for k, bias in enumerate((b_one, b_two, b_three)):
        eye = lax.broadcasted_iota(jnp.int32, (c, c), 0) == lax.broadcasted_iota(jnp.int32, (c, c), 1)
        column = jnp.sum(jnp.where(eye, bias[...], 0.0), axis=1, keepdims=True)
        cols[k] = jnp.broadcast_to(column, (c, w))

    lo, hi = pl.ds(0, w), pl.ds(w, w)

    def slot(t):
        return pl.ds(t * c, c)

    def row_copies(act, stage, f):
        up = pltpu.make_async_remote_copy(
            src_ref=act.at[f, slot(1), lo], dst_ref=act.at[f, slot(half + 1), hi],
            send_sem=row_send.at[stage, f, 0], recv_sem=row_recv.at[stage, f, 0],
            device_id=(clip, band - 1), device_id_type=MESH)
        down = pltpu.make_async_remote_copy(
            src_ref=act.at[f, slot(half), hi], dst_ref=act.at[f, slot(0), lo],
            send_sem=row_send.at[stage, f, 1], recv_sem=row_recv.at[stage, f, 1],
            device_id=(clip, band + 1), device_id_type=MESH)
        return up, down

    def send_rows(act, stage, f):
        up, down = row_copies(act, stage, f)
        pl.when(has_up)(up.start)
        pl.when(has_down)(down.start)

        @pl.when(jnp.logical_not(has_up))
        def _():
            act[f, slot(0), lo] = jnp.zeros((c, w), BF16)

        @pl.when(jnp.logical_not(has_down))
        def _():
            act[f, slot(half + 1), hi] = jnp.zeros((c, w), BF16)

        act[f, slot(half + 1), lo] = act[f, slot(1), hi]
        act[f, slot(0), hi] = act[f, slot(half), lo]

    def clip_copies(s):
        back = pltpu.make_async_remote_copy(
            src_ref=act_three.at[s, slot(1)], dst_ref=act_three.at[s, slot(frames + 1)],
            send_sem=clip_send.at[0, s], recv_sem=clip_recv.at[0, s],
            device_id=(clip - 1, band), device_id_type=MESH)
        ahead = pltpu.make_async_remote_copy(
            src_ref=act_three.at[s, slot(frames)], dst_ref=act_three.at[s, slot(0)],
            send_sem=clip_send.at[1, s], recv_sem=clip_recv.at[1, s],
            device_id=(clip + 1, band), device_id_type=MESH)
        return back, ahead

    def activate(f, s):
        act_one[f, pl.ds(pl.multiple_of((s + 1) * c, c), c), :] = silu(x[f, s].astype(F32)).astype(BF16)

    lane = lax.broadcasted_iota(jnp.int32, (n, w), 1)
    not_first, not_last = lane > 0, lane < w - 1

    def conv_slab(mat, act, stage, f, s):
        window = act[f, pl.ds(pl.multiple_of(s * c, c), 3 * c), :]
        for part in range(PARTS):
            rows = pl.ds(part * n, n)
            product = jnp.dot(mat[part], window, preferred_element_type=F32)
            bias = cols[stage, rows, :]
            for k in range(2):
                lanes = pl.ds(k * w, w)
                cut = slice(k * w, (k + 1) * w)
                left = jnp.where(not_first, pltpu.roll(product[:n, cut], 1, 1), 0.0)
                right = jnp.where(not_last, pltpu.roll(product[2 * n:, cut], w - 1, 1), 0.0)
                total = x[f, s, rows, lanes].astype(F32) + bias + (left + product[n:2 * n, cut] + right)
                rounded = total.astype(BF16)
                x[f, s, rows, lanes] = rounded
                active = silu(rounded.astype(F32)).astype(BF16)
                if stage == 0:
                    act_two[f, pl.ds(pl.multiple_of((s + 1) * c + part * n, 16), n), lanes] = active
                else:
                    act_three[s, pl.ds(pl.multiple_of((f + 1) * c + part * n, 16), n), lanes] = active

    def conv(stage, f, other=None):
        mat, act = (mat_one, act_one) if stage == 0 else (mat_two, act_two)

        def step(i, carry):
            @pl.when(i == half - 2)
            def _():
                up, down = row_copies(act, stage, f)
                pl.when(has_down)(up.wait_recv)
                pl.when(has_up)(down.wait_recv)

            s = jnp.where(i < half - 2, i + 1, jnp.where(i == half - 2, 0, half - 1))
            if other is not None:
                activate(other, i)
            conv_slab(mat, act, stage, f, s)
            if stage == 1:
                back, ahead = clip_copies(s)
                pl.when(jnp.logical_and(f == 0, has_prev))(back.start)
                pl.when(jnp.logical_and(f == frames - 1, has_next))(ahead.start)
            return carry

        if other is not None:
            for copy in load_x(other):
                copy.wait()
        lax.fori_loop(0, half, step, 0)
        if other is not None:
            send_rows(act_one, 0, other)
        if stage == 0:
            send_rows(act_two, 1, f)

    for copy in load_x(order[0]):
        copy.wait()

    def first_step(s, carry):
        activate(order[0], s)
        return carry

    lax.fori_loop(0, half, first_step, 0)
    send_rows(act_one, 0, order[0])

    def pack(raw, mat):
        for part in range(PARTS):
            for j in range(3):
                mat[part, pl.ds(j * n, n), :] = jnp.concatenate(
                    [raw[i, j, pl.ds(part * n, n), :] for i in range(3)], axis=1)

    for copy in loads_one:
        copy.wait()
    pack(raw_one, mat_one)

    conv(0, order[0], order[1])
    load_two.wait()
    pack(raw_two, mat_two)
    load_mix.wait()
    mat_mix[...] = jnp.concatenate([raw_mix[k] for k in range(3)], axis=1)

    for k, f in enumerate(order):
        if k + 1 < frames:
            conv(0, order[k + 1], order[k + 2] if k + 2 < frames else None)
        conv(1, f)

    @pl.when(jnp.logical_not(has_prev))
    def _():
        act_three[:, slot(0), :] = jnp.zeros((half, c, wide), BF16)

    @pl.when(jnp.logical_not(has_next))
    def _():
        act_three[:, slot(frames + 1), :] = jnp.zeros((half, c, wide), BF16)

    def out_copies(f, s):
        return [
            pltpu.make_async_copy(
                x.at[f, s, :, pl.ds(k * w, w)], out.at[f, s + k * half], o_sem.at[f, s, k])
            for k in range(2)
        ]

    def temporal(f, waits):
        def step(s, carry):
            back, ahead = clip_copies(s)
            if waits:
                pl.when(jnp.logical_and(f == frames - 1, has_next))(back.wait_recv)
                pl.when(jnp.logical_and(f == 0, has_prev))(ahead.wait_recv)
            window = act_three[s, pl.ds(pl.multiple_of(f * c, c), 3 * c), :]
            product = jnp.dot(mat_mix[...], window, preferred_element_type=F32)
            for k in range(2):
                lanes = pl.ds(k * w, w)
                total = x[f, s, :, lanes].astype(F32) + cols[2] + product[:, k * w:(k + 1) * w]
                x[f, s, :, lanes] = total.astype(BF16)
            start_all(out_copies(f, s))
            return carry

        lax.fori_loop(0, half, step, 0)

    for f in order[2:]:
        temporal(f, False)
    temporal(order[1], True)
    temporal(order[0], True)

    def finish(s, carry):
        for f in range(frames):
            for copy in out_copies(f, s):
                copy.wait()
        back, ahead = clip_copies(s)
        pl.when(has_prev)(back.wait_send)
        pl.when(has_next)(ahead.wait_send)
        return carry

    lax.fori_loop(0, half, finish, 0)
    for stage, act in ((0, act_one), (1, act_two)):
        for f in range(frames):
            up, down = row_copies(act, stage, f)
            pl.when(has_up)(up.wait_send)
            pl.when(has_down)(down.wait_send)


def body(clips, bands, video, spatial_one, spatial_two, temporal_mix, bias_one, bias_two, bias_three):
    frames, rows, c, w = video.shape
    half = rows // 2
    anywhere = pl.BlockSpec(memory_space=pl.ANY)
    vmem = pl.BlockSpec(memory_space=pltpu.VMEM)
    act = pltpu.VMEM((frames, (half + 2) * c, 2 * w), BF16)
    flops = 2 * frames * rows * w * c * c * 21
    return pl.pallas_call(
        functools.partial(kernel, clips, bands),
        out_shape=jax.ShapeDtypeStruct(video.shape, BF16),
        in_specs=[anywhere] * 4 + [vmem] * 3,
        out_specs=anywhere,
        scratch_shapes=[
            pltpu.VMEM(spatial_one.shape, BF16),
            pltpu.VMEM(spatial_two.shape, BF16),
            pltpu.VMEM(temporal_mix.shape, BF16),
            pltpu.VMEM((PARTS, 3 * c // PARTS, 3 * c), BF16),
            pltpu.VMEM((PARTS, 3 * c // PARTS, 3 * c), BF16),
            pltpu.VMEM((c, 3 * c), BF16),
            pltpu.VMEM((3, c, w), F32),
            pltpu.VMEM((frames, half, c, 2 * w), BF16),
            act,
            act,
            pltpu.VMEM((half, (frames + 2) * c, 2 * w), BF16),
            pltpu.SemaphoreType.DMA((5,)),
            pltpu.SemaphoreType.DMA((frames, 2)),
            pltpu.SemaphoreType.DMA((frames, half, 2)),
            pltpu.SemaphoreType.DMA((2, frames, 2)),
            pltpu.SemaphoreType.DMA((2, frames, 2)),
            pltpu.SemaphoreType.DMA((2, half)),
            pltpu.SemaphoreType.DMA((2, half)),
        ],
        cost_estimate=pl.CostEstimate(flops=flops, bytes_accessed=4 * video.size, transcendentals=0),
        compiler_params=pltpu.CompilerParams(
            collective_id=0, has_side_effects=True, vmem_limit_bytes=62 * 2**20),
    )(
        video, spatial_one, spatial_two, temporal_mix,
        bias_one.reshape(1, c), bias_two.reshape(1, c), bias_three.reshape(1, c),
    )


def solution(mesh):
    placed = (P("clip", "row", None, None), P(), P(), P(), P(), P(), P())
    return jax.shard_map(
        functools.partial(body, mesh.shape["clip"], mesh.shape["row"]),
        mesh=mesh, in_specs=placed, out_specs=P("clip", "row", None, None), check_vma=False,
    )
```

time: 97.4 us -> 51.5 us (0.53)
  the two profiles are of different devices: /device:TPU:14 before, /device:TPU:0 now
where the time goes in v1:
time: 51.5 us; the launch traced here: 51.3 us
  Pallas kernels  44.1 us (86%)
  local copies, waits for them, and re-layouts  7.17 us (14%)
    pallas_call x1, Pallas kernels, body(): pl.pallas_call(functools.partial(kernel, clips, bands), out_shape=jax.Sha...  44.1 us
    unnamed x1, local copies, waits for them, and re-layouts  3.41 us
    reshape x1, local copies, waits for them, and re-layouts, body(): bias_three.reshape(1, c)  1.26 us
    reshape x1, local copies, waits for them, and re-layouts, body(): bias_two.reshape(1, c)  1.26 us
    reshape x1, local copies, waits for them, and re-layouts, body(): bias_one.reshape(1, c)  1.24 us

profile of v1, /device:TPU:0, one launch (start us, length us, event | category | flops | bytes accessed | tf_op | source)
XLA Modules:
  0.0 51.3 jit_solution(15318307926264031826)
XLA Ops:
  0.0 1.2 %reshape.9.b_one = f32[1,320]{1,0:T(1,128)} reshape(f32[320]{0:T(512)} %param.11) | data formatting | bytes 2560 | tf_op jit(solution)/shard_map/reshape | solution.py:296
  1.2 1.3 %reshape.10.b_two = f32[1,320]{1,0:T(1,128)} reshape(f32[320]{0:T(512)} %param.12) | data formatting | bytes 2560 | tf_op jit(solution)/shard_map/reshape | solution.py:296
  2.5 1.3 %reshape.11.b_three = f32[1,320]{1,0:T(1,128)} reshape(f32[320]{0:T(512)} %param.13) | data formatting | bytes 2560 | tf_op jit(solution)/shard_map/reshape | solution.py:296
  3.8 44.1 %shard_map.73 = bf16[4,8,320,128]{3,2,1,0:T(8,128)(2,1)} custom-call(bf16[4,8,320,128]{3,2,1,0:T(8,128)(2,1)} %video.1, bf16[3,3,320,320]{3,2,1,0:T(8,128)(2,1)} %w_one.1, bf16[3,3,320,320]{3,2,1,0:T(8,128)(2,1)} %w_two.1, bf16[3,320,320]{2,1,0:T(8,128)(2,1)} %w_mix.1, f32[1,320]{1,0:T(1,128)} %reshape.9.b_one, f32[1,320]{1,0:T(1,128)} %reshape.10.b_two, ...), custom_call_target="tpu_custom_call" | custom-call | flops 17616076800 | bytes 5242880 | tf_op jit(solution)/shard_map/pallas_call | solution.py:266
  47.9 3.4 %copy.9 = bf16[4,8,320,128]{3,2,1,0:T(8,128)(2,1)} copy(bf16[4,8,320,128]{3,2,1,0:T(8,128)(2,1)} %shard_map.73) | data formatting | bytes 5242880

commit v2 on v1

--- a/solution.py
+++ b/solution.py
@@ -9,7 +9,7 @@
 
 BF16, F32 = jnp.bfloat16, jnp.float32
 MESH = pl.DeviceIdType.MESH
-PARTS = 2
+CHUNK = 64
 
 
 def silu(v):
@@ -19,12 +19,12 @@
 
 def kernel(
     clips, bands, video, w_one, w_two, w_mix, b_one, b_two, b_three, out,
-    raw_one, raw_two, raw_mix, mat_one, mat_two, mat_mix, cols, x, act_one, act_two, act_three,
+    raw_one, raw_two, raw_mix, mat_one, mat_two, mat_mix, cols, x, act_one, act_two, act_three, prod_a, prod_b,
     w_sem, x_sem, o_sem, row_send, row_recv, clip_send, clip_recv,
 ):
     frames, half, c, wide = x.shape
     w = wide // 2
-    n = c // PARTS
+    n = CHUNK
     clip, band = lax.axis_index("clip"), lax.axis_index("row")
     has_up, has_down = band > 0, band < bands - 1
     has_prev, has_next = clip > 0, clip < clips - 1
@@ -70,7 +70,7 @@
 
     for k, bias in enumerate((b_one, b_two, b_three)):
         eye = lax.broadcasted_iota(jnp.int32, (c, c), 0) == lax.broadcasted_iota(jnp.int32, (c, c), 1)
-        column = jnp.sum(jnp.where(eye, bias[...], 0.0), axis=1, keepdims=True)
+        column = jnp.sum(jnp.where(eye, bias[...][None, :], 0.0), axis=1, keepdims=True)
         cols[k] = jnp.broadcast_to(column, (c, w))
 
     lo, hi = pl.ds(0, w), pl.ds(w, w)
@@ -122,54 +122,56 @@
     lane = lax.broadcasted_iota(jnp.int32, (n, w), 1)
     not_first, not_last = lane > 0, lane < w - 1
 
-    def conv_slab(mat, act, stage, f, s):
-        window = act[f, pl.ds(pl.multiple_of(s * c, c), 3 * c), :]
-        for part in range(PARTS):
+    def multiply(stage, f, s, product):
+        mat, act = ((mat_one, act_one), (mat_two, act_two))[stage]
+        window = act[f, pl.ds(s * c, 3 * c), :]
+        product[...] = jnp.dot(mat[...], window, preferred_element_type=F32)
+
+    def finish_slab(stage, f, s, product):
+        for part in range(c // n):
             rows = pl.ds(part * n, n)
-            product = jnp.dot(mat[part], window, preferred_element_type=F32)
             bias = cols[stage, rows, :]
-            for k in range(2):
-                lanes = pl.ds(k * w, w)
-                cut = slice(k * w, (k + 1) * w)
-                left = jnp.where(not_first, pltpu.roll(product[:n, cut], 1, 1), 0.0)
-                right = jnp.where(not_last, pltpu.roll(product[2 * n:, cut], w - 1, 1), 0.0)
-                total = x[f, s, rows, lanes].astype(F32) + bias + (left + product[n:2 * n, cut] + right)
+            for lanes in (lo, hi):
+                left = jnp.where(not_first, pltpu.roll(product[rows, lanes], 1, 1), 0.0)
+                right = jnp.where(not_last, pltpu.roll(product[pl.ds(2 * c + part * n, n), lanes], w - 1, 1), 0.0)
+                middle = product[pl.ds(c + part * n, n), lanes]
+                total = x[f, s, rows, lanes].astype(F32) + bias + (left + middle + right)
                 rounded = total.astype(BF16)
                 x[f, s, rows, lanes] = rounded
                 active = silu(rounded.astype(F32)).astype(BF16)
                 if stage == 0:
-                    act_two[f, pl.ds(pl.multiple_of((s + 1) * c + part * n, 16), n), lanes] = active
+                    act_two[f, pl.ds((s + 1) * c + part * n, n), lanes] = active
                 else:
                     act_three[s, pl.ds(pl.multiple_of((f + 1) * c + part * n, 16), n), lanes] = active
-
-    def conv(stage, f, other=None):
-        mat, act = (mat_one, act_one) if stage == 0 else (mat_two, act_two)
-
-        def step(i, carry):
-            @pl.when(i == half - 2)
-            def _():
+        if stage == 1:
+            back, ahead = clip_copies(s)
+            pl.when(jnp.logical_and(f == 0, has_prev))(back.start)
+            pl.when(jnp.logical_and(f == frames - 1, has_next))(ahead.start)
+
+    products = (prod_a, prod_b)
+    row_order = list(range(1, half - 1)) + [0, half - 1]
+
+    def conv(stage, f, pending, other=None):
+        act = act_one if stage == 0 else act_two
+        if other is not None:
+            for copy in load_x(other):
+                copy.wait()
+        for i, s in enumerate(row_order):
+            if i == half - 2:
                 up, down = row_copies(act, stage, f)
                 pl.when(has_down)(up.wait_recv)
                 pl.when(has_up)(down.wait_recv)
-
-            s = jnp.where(i < half - 2, i + 1, jnp.where(i == half - 2, 0, half - 1))
+            multiply(stage, f, s, products[i % 2])
+            if pending is not None:
+                finish_slab(*pending)
+                if i == 0 and pending[0] == 0:
+                    send_rows(act_two, 1, pending[1])
             if other is not None:
                 activate(other, i)
-            conv_slab(mat, act, stage, f, s)
-            if stage == 1:
-                back, ahead = clip_copies(s)
-                pl.when(jnp.logical_and(f == 0, has_prev))(back.start)
-                pl.when(jnp.logical_and(f == frames - 1, has_next))(ahead.start)
-            return carry
-
-        if other is not None:
-            for copy in load_x(other):
-                copy.wait()
-        lax.fori_loop(0, half, step, 0)
+            pending = (stage, f, s, products[i % 2])
         if other is not None:
             send_rows(act_one, 0, other)
-        if stage == 0:
-            send_rows(act_two, 1, f)
+        return pending
 
     for copy in load_x(order[0]):
         copy.wait()
@@ -182,16 +184,14 @@
     send_rows(act_one, 0, order[0])
 
     def pack(raw, mat):
-        for part in range(PARTS):
-            for j in range(3):
-                mat[part, pl.ds(j * n, n), :] = jnp.concatenate(
-                    [raw[i, j, pl.ds(part * n, n), :] for i in range(3)], axis=1)
+        for j in range(3):
+            mat[pl.ds(j * c, c), :] = jnp.concatenate([raw[i, j] for i in range(3)], axis=1)
 
     for copy in loads_one:
         copy.wait()
     pack(raw_one, mat_one)
 
-    conv(0, order[0], order[1])
+    pending = conv(0, order[0], None, order[1])
     load_two.wait()
     pack(raw_two, mat_two)
     load_mix.wait()
@@ -199,8 +199,13 @@
 
     for k, f in enumerate(order):
         if k + 1 < frames:
-            conv(0, order[k + 1], order[k + 2] if k + 2 < frames else None)
-        conv(1, f)
+            pending = conv(0, order[k + 1], pending, order[k + 2] if k + 2 < frames else None)
+        elif pending[0] == 0:
+            finish_slab(*pending)
+            send_rows(act_two, 1, pending[1])
+            pending = None
+        pending = conv(1, f, pending)
+    finish_slab(*pending)
 
     @pl.when(jnp.logical_not(has_prev))
     def _():
@@ -272,14 +277,16 @@
             pltpu.VMEM(spatial_one.shape, BF16),
             pltpu.VMEM(spatial_two.shape, BF16),
             pltpu.VMEM(temporal_mix.shape, BF16),
-            pltpu.VMEM((PARTS, 3 * c // PARTS, 3 * c), BF16),
-            pltpu.VMEM((PARTS, 3 * c // PARTS, 3 * c), BF16),
+            pltpu.VMEM((3 * c, 3 * c), BF16),
+            pltpu.VMEM((3 * c, 3 * c), BF16),
             pltpu.VMEM((c, 3 * c), BF16),
             pltpu.VMEM((3, c, w), F32),
             pltpu.VMEM((frames, half, c, 2 * w), BF16),
             act,
             act,
             pltpu.VMEM((half, (frames + 2) * c, 2 * w), BF16),
+            pltpu.VMEM((3 * c, 2 * w), F32),
+            pltpu.VMEM((3 * c, 2 * w), F32),
             pltpu.SemaphoreType.DMA((5,)),
             pltpu.SemaphoreType.DMA((frames, 2)),
             pltpu.SemaphoreType.DMA((frames, half, 2)),
@@ -293,7 +300,7 @@
             collective_id=0, has_side_effects=True, vmem_limit_bytes=62 * 2**20),
     )(
         video, spatial_one, spatial_two, temporal_mix,
-        bias_one.reshape(1, c), bias_two.reshape(1, c), bias_three.reshape(1, c),
+        bias_one, bias_two, bias_three,
     )
 
 

time: 51.5 us -> 48.4 us (0.940)
  local copies, waits for them, and re-layouts: 7.17 us -> 3.41 us
  Pallas kernels: 44.1 us -> 44.9 us
    reshape x3 -> x0, local copies, waits for them, and re-layouts: 3.76 us -> none  [the longest x1 1.26 us: body(): bias_three.reshape(1, c)]
    pallas_call x1, Pallas kernels: 44.1 us -> 44.9 us  [body(): pl.pallas_call(functools.partial(kernel, clips, bands), out_shape=jax.Sha...]
where the time goes in v2:
time: 48.4 us; the launch traced here: 48.3 us
  Pallas kernels  44.9 us (93%)
  local copies, waits for them, and re-layouts  3.41 us (7%)
    pallas_call x1, Pallas kernels, body(): pl.pallas_call(functools.partial(kernel, clips, bands), out_shape=jax.Sha...  44.9 us
    unnamed x1, local copies, waits for them, and re-layouts  3.41 us

profile of v2, /device:TPU:0, one launch (start us, length us, event | category | flops | bytes accessed | tf_op | source)
XLA Modules:
  0.0 48.3 jit_solution(18276257251238385482)
XLA Ops:
  0.0 44.9 %shard_map.73 = bf16[4,8,320,128]{3,2,1,0:T(8,128)(2,1)} custom-call(bf16[4,8,320,128]{3,2,1,0:T(8,128)(2,1)} %video.1, bf16[3,3,320,320]{3,2,1,0:T(8,128)(2,1)} %w_one.1, bf16[3,3,320,320]{3,2,1,0:T(8,128)(2,1)} %w_two.1, bf16[3,320,320]{2,1,0:T(8,128)(2,1)} %w_mix.1, f32[320]{0:T(512)} %b_one.1, f32[320]{0:T(512)} %b_two.1, f32[320]{0:T(512)} %b_three.1), custom_call_target="tpu_custom_call" | custom-call | flops 17616076800 | bytes 5242880 | tf_op jit(solution)/shard_map/pallas_call | solution.py:271
  44.9 3.4 %copy.9 = bf16[4,8,320,128]{3,2,1,0:T(8,128)(2,1)} copy(bf16[4,8,320,128]{3,2,1,0:T(8,128)(2,1)} %shard_map.73) | data formatting | bytes 5242880
